TPU v7x, 32 devices: a whole 2x2x4 slice. The times are simulated.
32 devices in a mesh: groups: 2 (over y), replica: 16 (over z, x, core).
Axes of the slice: x: 2, y: 2, z: 4, core: 2. Of those that a mesh axis runs over, the one named last changes fastest.
Arguments:
- queries: bfloat16 [64, 4, 4096], P(('groups', 'replica')), parts along dimension 0, may hold values from -4 to 4
- keys: bfloat16 [64, 4, 4096], P(('groups', 'replica')), parts along dimension 0, may hold values from -4 to 4
- values: bfloat16 [64, 4, 4096], P(('groups', 'replica')), parts along dimension 0, may hold values from -6 to 6
- gate_input: bfloat16 [64, 4, 4096], P(('groups', 'replica')), parts along dimension 0, may hold values from -6 to 6
- decay_rate: float32 [32], replicated, may hold values from 0.05 to 1.5
- norm_gain: float32 [4096], replicated, may hold values from 0.1 to 1.9
- out_weight: bfloat16 [4096, 3072], P('replica'), may hold values from -0.09375 to 0.09375
- prompt_states: bfloat16 [8, 4096, 128], P('groups', 'replica'), parts along dimension 0, may hold values from -4 to 4
- group_sizes: int32 [8], P('groups'), parts along dimension 0, may hold values from 1 to 16, 32 in all
Outputs:
- mixed: bfloat16 [64, 4, 3072], P(('groups', 'replica')), parts along dimension 0
There are 2 independent parts, one for each index of `groups`. A program takes and returns all parts, laid end to end along the dimension named above; an argument that names none is the same for every part. Nothing has to cross between parts.
Inputs may be any that keep to these rules, and one draw needn't show every extreme that they name: `group_sizes`: the group sizes sum to 32, and the largest is exactly 16.
All inputs are finite; a program needn't handle non-finite values.
Results may differ from a plain program's by a relative error of at most 0.005.
Values may be sent and summed in bfloat16 or wider, within the bound.
A program may use at most 64 MiB of HBM per device.

v0:
```python
import jax
import jax.numpy as jnp
from jax import lax
from jax.sharding import PartitionSpec as P


def on_device(
    queries, keys, values, gate_input, decay_rate, norm_gain, out_weight, prompt_states, group_sizes
):
    replicas = lax.axis_size("replica")
    rows_local, steps_count, features = queries.shape
    head_size = prompt_states.shape[2]
    head_count = features // head_size
    share = prompt_states.shape[1]
    rows_total = rows_local * replicas
    ends = jnp.cumsum(group_sizes)
    row_ids = jnp.arange(rows_total, dtype=jnp.int32)
    owners = jnp.sum((row_ids[:, None] >= ends[None, :]).astype(jnp.int32), axis=1)
    q_four = queries.reshape(rows_local, steps_count, head_count, head_size)
    k_four = keys.reshape(rows_local, steps_count, head_count, head_size)
    v_four = values.astype(jnp.float32).reshape(rows_local, steps_count, head_count, head_size)
    piece = min(share, head_size)
    pieces_here = share // piece
    per_head = head_size // piece
    query_parts = queries.reshape(rows_local, steps_count, replicas, share)
    held_queries = lax.all_to_all(query_parts, "replica", split_axis=2, concat_axis=0, tiled=True)
    held_queries = held_queries.reshape(rows_total, steps_count, pieces_here, piece)
    held_states = jnp.take(prompt_states, owners, axis=0).reshape(
        rows_total, pieces_here, piece, head_size
    )
    partial_value = jnp.einsum(
        "rtcd,rcde->rtce", held_queries, held_states, preferred_element_type=jnp.float32
    )
    partial_value = partial_value.reshape(replicas, rows_local, steps_count, pieces_here, head_size)
    returned = lax.all_to_all(partial_value, "replica", split_axis=0, concat_axis=0, tiled=True)
    returned = jnp.moveaxis(returned, 0, 2)
    returned = returned.reshape(rows_local, steps_count, head_count, per_head, head_size)
    prompt_read = jnp.sum(returned, axis=3)
    times = jnp.arange(1, steps_count + 1).astype(jnp.float32)
    lead = jnp.exp(-times[:, None] * decay_rate[None, :])
    gap = times[:, None] - times[None, :]
    weights_mix = jnp.where(
        gap[None] >= 0.0, jnp.exp(-jnp.maximum(gap, 0.0)[None] * decay_rate[:, None, None]), 0.0
    )
    scores = jnp.einsum("rthd,rshd->rhts", q_four, k_four, preferred_element_type=jnp.float32)
    recent = jnp.einsum(
        "rhts,rshe->rthe", scores * weights_mix[None], v_four, precision=lax.Precision.HIGHEST
    )
    attention = lead[None, :, :, None] * prompt_read + recent
    attention = attention.reshape(rows_local, steps_count, features)
    mean_square = jnp.mean(attention * attention, axis=-1, keepdims=True)
    gate = jax.nn.sigmoid(gate_input.astype(jnp.float32))
    hidden = (attention * lax.rsqrt(mean_square + 1e-06) * norm_gain * gate).astype(jnp.bfloat16)
    hidden = hidden.reshape(rows_local * steps_count, features)
    columns_held = lax.all_to_all(hidden, "replica", split_axis=1, concat_axis=0, tiled=True)
    mixed = lax.psum_scatter(
        jnp.dot(columns_held, out_weight, preferred_element_type=jnp.float32),
        "replica",
        scatter_dimension=0,
        tiled=True,
    )
    return mixed.astype(jnp.bfloat16).reshape(rows_local, steps_count, out_weight.shape[1])


def solution(mesh):
    in_specs = (
        P(("groups", "replica"), None, None),
        P(("groups", "replica"), None, None),
        P(("groups", "replica"), None, None),
        P(("groups", "replica"), None, None),
        P(),
        P(),
        P("replica", None),
        P("groups", "replica", None),
        P("groups"),
    )
    out_specs = P(("groups", "replica"), None, None)
    return jax.shard_map(
        on_device, mesh=mesh, in_specs=in_specs, out_specs=out_specs, check_vma=False
    )
```

profile of v0, /device:TPU:0, one launch (start us, length us, event | category | flops | bytes accessed | tf_op | source)
XLA Modules:
  0.0 114.6 jit_solution(6417857061044807749)
XLA Ops:
  6.5 0.0 copy-start
  6.5 1.6 %copy.47 = bf16[2,1,16,4,256]{4,3,1,0,2:T(4,128)(2,1)} copy(bf16[2,1,16,4,256]{4,3,2,1,0:T(4,128)(2,1)} %bitcast.54) | data formatting | bytes 131072 | tf_op jit(solution)/shard_map/reshape | solution.py:25
  8.1 7.4 %all-to-all-start = ((bf16[2,4,16,256]{3,1,0,2:T(4,128)(2,1)}), bf16[2,4,16,256]{3,1,0,2:T(4,128)(2,1)S(1)}, u32[]{:S(2)}, u32[]{:S(2)}) async-start(bf16[2,4,16,256]{3,1,0,2:T(4,128)(2,1)} %bitcast.51), calls=%async_computation | async-start | bytes 131072 | tf_op jit(solution)/shard_map/all_to_all | solution.py:26
  15.5 0.8 reduce-window.8
  16.3 0.1 convert_reduce_fusion
  16.4 0.1 fusion.12
  16.5 0.1 subtract_compare_fusion
  16.6 0.8 exponential_select_fusion
  17.4 3.1 %gather_fusion = bf16[32,256,128]{2,1,0:T(8,128)(2,1)} fusion(bf16[4,256,128]{2,1,0:T(8,128)(2,1)} %param.16, s32[1024]{0:T(1024)S(1)} %pad_clamp_fusion), kind=kCustom, calls=%fused_computation | custom fusion | bytes 4194432 | tf_op jit(solution)/shard_map/jit(_take)/gather | solution.py:28
  20.5 1.9 %all-to-all-done = bf16[2,4,16,256]{3,1,0,2:T(4,128)(2,1)S(1)} async-done(((bf16[2,4,16,256]{3,1,0,2:T(4,128)(2,1)}), bf16[2,4,16,256]{3,1,0,2:T(4,128)(2,1)S(1)}, u32[]{:S(2)}, u32[]{:S(2)}) %all-to-all-start) | async-done | bytes 65568 | tf_op jit(solution)/shard_map/all_to_all | solution.py:26
  22.4 0.0 copy-start.5
  22.4 0.0 copy-start.1
  22.4 0.0 copy-start.2
  22.4 0.0 copy-start.6
  22.4 0.0 copy-start.3
  22.4 0.0 copy-start.4
  22.4 3.0 %fusion = f32[32,2,128,4]{2,3,1,0:T(4,128)} fusion(bf16[32,4,2,128]{3,1,2,0:T(4,128)(2,1)S(1)} %bitcast.56, bf16[32,2,128,128]{3,2,1,0:T(8,128)(2,1)} %bitcast.52, pred[32]{0:T(512)(128)(4,1)S(1)} %compare_and_fusion), kind=kOutput, calls=%fused_computation.1 | convolution fusion | flops 9437184 | bytes 2293792 | tf_op jit(solution)/shard_map/rtcd,rcde->rtce/dot_general | solution.py:31
  25.5 4.1 %all-to-all-start.1 = ((f32[16,2,4,2,128]{4,2,3,1,0:T(4,128)}), f32[16,2,4,2,128]{4,2,3,1,0:T(4,128)S(1)}, u32[]{:S(2)}, u32[]{:S(2)}) async-start(f32[16,2,4,2,128]{4,2,3,1,0:T(4,128)} %bitcast.9), calls=%async_computation.1 | async-start | bytes 262144 | tf_op jit(solution)/shard_map/all_to_all | solution.py:35
  29.6 0.0 reduce-scatter.2.cloned.1.call-start
  29.7 0.0 copy-done.5
  29.7 0.1 multiply_exponential_fusion
  29.7 0.1 copy.37
  29.8 0.0 copy-done.1
  29.8 0.0 copy-done.2
  29.8 0.2 convolution_multiply_fusion
  30.0 7.5 %all-to-all-done.1 = f32[16,2,4,2,128]{4,2,3,1,0:T(4,128)S(1)} async-done(((f32[16,2,4,2,128]{4,2,3,1,0:T(4,128)}), f32[16,2,4,2,128]{4,2,3,1,0:T(4,128)S(1)}, u32[]{:S(2)}, u32[]{:S(2)}) %all-to-all-start.1) | async-done | bytes 131104 | tf_op jit(solution)/shard_map/all_to_all | solution.py:35
  37.6 0.0 copy-done.6
  37.6 0.4 multiply_reduce_fusion
  38.0 0.0 copy-done.3
  38.0 0.0 copy-done.4
  38.0 0.1 fusion.6
  38.2 9.5 %all_to_all.39 = bf16[8,16,256]{2,0,1:T(8,128)(2,1)S(1)} all-to-all(bf16[8,16,256]{2,0,1:T(8,128)(2,1)S(1)} %copy.44), channel_id=1, replica_groups=mesh['groups'=2,'replica'=16] {'replica'}, dimensions={1} | all-to-all | bytes 131072 | tf_op jit(solution)/shard_map/all_to_all | solution.py:55
  47.7 0.0 copy-done
  47.7 1.5 %fusion.7 = f32[128,3072]{1,0:T(8,128)} fusion(bf16[256,3072]{1,0:T(8,128)(2,1)S(1)} %copy-done, bf16[8,16,256]{2,0,1:T(8,128)(2,1)S(1)} %all_to_all.39), kind=kOutput, calls=%fused_computation.14 | convolution fusion | flops 201326592 | bytes 3211264 | tf_op jit(solution)/shard_map/dot_general | solution.py:57
  49.2 0.0 reduce-scatter.2.cloned.1.call-update
  49.3 57.0 %reduce-scatter.2.cloned.1.call-done = f32[8,3072]{1,0:T(8,128)} async-done(((f32[128,3072]{1,0:T(8,128)}), f32[8,3072]{1,0:T(8,128)}) %reduce-scatter.2.cloned.1.call-update) | async-done | bytes 98320 | tf_op jit(solution)/shard_map/reduce_scatter | solution.py:56
  106.2 0.9 convert_element_type.35
  107.1 0.6 reshape.202
  (9 shorter events, 0.1 us)
Async XLA Ops:
  6.5 41.2 %copy-start = (bf16[256,3072]{1,0:T(8,128)(2,1)S(1)}, bf16[256,3072]{1,0:T(8,128)(2,1)}, u32[]{:S(2)}) copy-start(bf16[256,3072]{1,0:T(8,128)(2,1)} %param.15) | copy-start | bytes 4718596
  8.1 14.3 %all-to-all-start = ((bf16[2,4,16,256]{3,1,0,2:T(4,128)(2,1)}), bf16[2,4,16,256]{3,1,0,2:T(4,128)(2,1)S(1)}, u32[]{:S(2)}, u32[]{:S(2)}) async-start(bf16[2,4,16,256]{3,1,0,2:T(4,128)(2,1)} %bitcast.51), calls=%async_computation | async-start | bytes 131072 | tf_op jit(solution)/shard_map/all_to_all | solution.py:26
  22.4 7.3 %copy-start.5 = (f32[32]{0:T(128)S(1)}, f32[32]{0:T(128)}, u32[]{:S(2)}) copy-start(f32[32]{0:T(128)} %param.13) | copy-start | bytes 388
  22.4 7.4 %copy-start.1 = (bf16[2,4,4096]{2,1,0:T(4,128)(2,1)S(1)}, bf16[2,4,4096]{2,1,0:T(4,128)(2,1)}, u32[]{:S(2)}) copy-start(bf16[2,4,4096]{2,1,0:T(4,128)(2,1)} %param.9) | copy-start | bytes 196612
  22.4 7.4 %copy-start.2 = (bf16[2,4,4096]{2,1,0:T(4,128)(2,1)S(1)}, bf16[2,4,4096]{2,1,0:T(4,128)(2,1)}, u32[]{:S(2)}) copy-start(bf16[2,4,4096]{2,1,0:T(4,128)(2,1)} %param.10) | copy-start | bytes 196612
  22.4 15.2 %copy-start.6 = (bf16[2,4,4096]{2,1,0:T(4,128)(2,1)S(1)}, bf16[2,4,4096]{2,1,0:T(4,128)(2,1)}, u32[]{:S(2)}) copy-start(bf16[2,4,4096]{2,1,0:T(4,128)(2,1)} %param.11) | copy-start | bytes 196612
  22.4 15.6 %copy-start.3 = (bf16[2,4,4096]{2,1,0:T(4,128)(2,1)S(1)}, bf16[2,4,4096]{2,1,0:T(4,128)(2,1)}, u32[]{:S(2)}) copy-start(bf16[2,4,4096]{2,1,0:T(4,128)(2,1)} %param.12) | copy-start | bytes 196612
  22.4 15.6 %copy-start.4 = (f32[4096]{0:T(1024)S(1)}, f32[4096]{0:T(1024)}, u32[]{:S(2)}) copy-start(f32[4096]{0:T(1024)} %param.14) | copy-start | bytes 49156
  25.5 12.1 %all-to-all-start.1 = ((f32[16,2,4,2,128]{4,2,3,1,0:T(4,128)}), f32[16,2,4,2,128]{4,2,3,1,0:T(4,128)S(1)}, u32[]{:S(2)}, u32[]{:S(2)}) async-start(f32[16,2,4,2,128]{4,2,3,1,0:T(4,128)} %bitcast.9), calls=%async_computation.1 | async-start | bytes 262144 | tf_op jit(solution)/shard_map/all_to_all | solution.py:35
  29.6 76.6 %reduce-scatter.2.cloned.1.call-start = ((), (), s32[]{:S(2)}) async-start(), calls=%async_computation.4 | async-start | bytes 1671168 | tf_op jit(solution)/shard_map/reduce_scatter | solution.py:56
Sparse Core Ops, SparseCore 0:
  49.4 56.8 reduce-scatter.1
where the time goes:
time: 115 us
  waiting for transfers between devices  66.4 us (58%)
  between operations  13.5 us (12%)
  starting transfers between devices  11.5 us (10%)
  blocking collectives  9.48 us (8%)
  local copies, waits for them, and re-layouts  5.53 us (5%)
  matrix products  5.22 us (5%)
  other arithmetic  2.95 us (3%)
    reduce_scatter x1, waiting for transfers between devices, on_device(): lax.psum_scatter(jnp.dot(columns_held, out_weight, preferred_element_type...  57 us
    all_to_all x1, blocking collectives, on_device(): lax.all_to_all(hidden, 'replica', split_axis=1, concat_axis=0, tiled=True)  9.48 us
    all_to_all x1, waiting for transfers between devices, on_device(): lax.all_to_all(partial_value, 'replica', split_axis=0, concat_axis=0, til...  7.49 us
    all_to_all x1, starting transfers between devices, on_device(): lax.all_to_all(query_parts, 'replica', split_axis=2, concat_axis=0, tiled...  7.36 us
    all_to_all x1, starting transfers between devices, on_device(): lax.all_to_all(partial_value, 'replica', split_axis=0, concat_axis=0, til...  4.14 us
    gather x1, local copies, waits for them, and re-layouts, on_device(): jnp.take(prompt_states, owners, axis=0)  3.1 us
    dot_general x1, matrix products, on_device(): jnp.einsum('rtcd,rcde->rtce', held_queries, held_states, preferred_elemen...  3.02 us
  transfers between devices with their start and end apart: 3, of which 3 were waited for; matrix products, arithmetic and copies ran while one was open for 5% of the time, Pallas kernels for 0%

commit v1 on v0

v1 whole, which is shorter than its diff:
```python
import functools

import jax
import jax.numpy as jnp
from jax import lax
from jax.experimental import pallas as pl
from jax.experimental.pallas import tpu as pltpu
from jax.sharding import PartitionSpec as P

MESH = pl.DeviceIdType.MESH
F32 = jnp.float32
BF16 = jnp.bfloat16


def kernel(
    chips,
    q_ref, k_ref, v_ref, g_ref, decay_ref, gain_ref, w_hbm, st_hbm, gs_ref,
    out_ref,
    stage, sbuf, rbuf, w_buf, st_buf, pbuf, precv, own, ss_send, ss_recv,
    local_sem, pair_send, pair_recv, x_send, x_recv, p_send, p_recv, s_send, s_recv,
):
    rows_local, steps, features = q_ref.shape
    tokens_local = rows_local * steps
    prompts, share, hd = st_hbm.shape
    wide = 2 * share
    heads_device = share // hd
    half = w_hbm.shape[1] // 2
    tokens = chips * tokens_local
    me = lax.axis_index("replica")
    chip = me // 2
    core = lax.rem(me, 2)
    partner = chip * 2 + 1 - core

    def peer(chip_index):
        return {"replica": lax.rem(chip_index + chips, chips) * 2 + core}

    w_own = pltpu.make_async_copy(w_hbm, w_buf.at[core], local_sem.at[0])
    st_own = pltpu.make_async_copy(st_hbm, st_buf.at[core], local_sem.at[1])
    st_own.start()
    w_own.start()

    barrier = pltpu.get_barrier_semaphore()
    pl.semaphore_signal(barrier, inc=1, device_id={"replica": partner}, device_id_type=MESH)
    for o in range(1, chips):
        pl.semaphore_signal(barrier, inc=1, device_id=peer(chip + o), device_id_type=MESH)

    for kind, ref in enumerate((q_ref, k_ref, v_ref, g_ref)):
        for r in range(rows_local):
            at = kind * tokens_local + r * steps
            stage[at:at + steps, :] = ref[r].astype(F32)
    for o in range(chips):
        off = pl.multiple_of(lax.rem(chip + o, chips) * wide, wide)
        block = stage[:, pl.ds(off, wide)].astype(BF16)
        if o == 0:
            rbuf[0] = block
        else:
            sbuf[o] = block

    pl.semaphore_wait(barrier, chips)

    x_copies = []
    for o in range(1, chips):
        copy = pltpu.make_async_remote_copy(
            src_ref=sbuf.at[o], dst_ref=rbuf.at[o], send_sem=x_send.at[o], recv_sem=x_recv.at[o],
            device_id=peer(chip + o), device_id_type=MESH,
        )
        copy.start()
        x_copies.append(copy)
    st_pair = pltpu.make_async_remote_copy(
        src_ref=st_hbm, dst_ref=st_buf.at[core], send_sem=pair_send.at[0], recv_sem=pair_recv.at[0],
        device_id={"replica": partner}, device_id_type=MESH,
    )
    st_pair.start()
    w_pair = pltpu.make_async_remote_copy(
        src_ref=w_hbm, dst_ref=w_buf.at[core], send_sem=pair_send.at[1], recv_sem=pair_recv.at[1],
        device_id={"replica": partner}, device_id_type=MESH,
    )
    w_pair.start()

    token = lax.broadcasted_iota(jnp.int32, (tokens, 1), 0)
    source = lax.rem(chip - token // tokens_local + chips, chips)
    row = (source * 2 + core) * rows_local + lax.rem(token, tokens_local) // steps
    step = lax.rem(token, steps)
    lead_time = (step + 1).astype(F32)
    ti = lax.broadcasted_iota(jnp.int32, (tokens, tokens), 0)
    si = lax.broadcasted_iota(jnp.int32, (tokens, tokens), 1)
    live = (ti // steps == si // steps) & (si <= ti)
    gap = jnp.maximum(ti - si, 0).astype(F32)
    masks = []
    start = jnp.int32(0)
    for p in range(prompts):
        end = start + gs_ref[p]
        masks.append((row >= start) & (row < end))
        start = end

    st_own.wait()
    st_pair.wait()
    for copy in x_copies:
        copy.wait()

    us = []
    square = jnp.zeros((tokens, 1), F32)
    for h in range(2 * heads_device):
        head = chip * 2 * heads_device + h
        cols = slice(h * hd, (h + 1) * hd)
        block = rbuf[:, :, cols].astype(F32)
        q, k, v, g = (
            block[:, i * tokens_local:(i + 1) * tokens_local, :].reshape(tokens, hd) for i in range(4)
        )
        decay = decay_ref[head]
        read = jnp.zeros((tokens, hd), F32)
        keys_at = (h % heads_device) * hd
        for p in range(prompts):
            state = st_buf[h // heads_device, p, keys_at:keys_at + hd, :]
            read += jnp.dot(
                jnp.where(masks[p], q, 0.0).astype(BF16), state, preferred_element_type=F32
            )
        scores = lax.dot_general(
            q.astype(BF16), k.astype(BF16), (((1,), (1,)), ((), ())), preferred_element_type=F32
        )
        scores = scores * jnp.where(live, jnp.exp(-gap * decay), 0.0)
        high = scores.astype(BF16)
        low = (scores - high.astype(F32)).astype(BF16)
        vb = v.astype(BF16)
        recent = jnp.dot(high, vb, preferred_element_type=F32) + jnp.dot(
            low, vb, preferred_element_type=F32
        )
        attention = jnp.exp(-lead_time * decay) * read + recent
        square += jnp.sum(attention * attention, axis=1, keepdims=True)
        gain = gain_ref[pl.ds(head, 1), :]
        us.append((attention * gain * jax.nn.sigmoid(g)).astype(BF16))

    ss_send[...] = jnp.broadcast_to(square, (tokens, 128)).reshape(chips, tokens_local, 128)
    s_copies = []
    for o in range(1, chips):
        copy = pltpu.make_async_remote_copy(
            src_ref=ss_send.at[o], dst_ref=ss_recv.at[o], send_sem=s_send.at[o], recv_sem=s_recv.at[o],
            device_id=peer(chip - o), device_id_type=MESH,
        )
        copy.start()
        s_copies.append(copy)

    u0 = jnp.concatenate(us[:heads_device], axis=1)
    u1 = jnp.concatenate(us[heads_device:], axis=1)
    w_own.wait()
    w_pair.wait()
    parts, tile = pbuf.shape[0], pbuf.shape[3]
    p_copies = []
    for c in range(parts):
        pieces = []
        for base in (0, half):
            at = slice(base + c * tile, base + (c + 1) * tile)
            y = jnp.dot(u0, w_buf[0, :, at], preferred_element_type=F32)
            y += jnp.dot(u1, w_buf[1, :, at], preferred_element_type=F32)
            pieces.append(y.reshape(chips, tokens_local, tile))
        both = jnp.concatenate(pieces, axis=1)
        own[c] = both[0]
        pbuf[c] = both.astype(BF16)
        for o in range(1, chips):
            copy = pltpu.make_async_remote_copy(
                src_ref=pbuf.at[c, o], dst_ref=precv.at[c, o],
                send_sem=p_send.at[c, o], recv_sem=p_recv.at[c, o],
                device_id=peer(chip - o), device_id_type=MESH,
            )
            copy.start()
            p_copies.append(copy)

    for copy in s_copies:
        copy.wait()
    total_square = ss_send[0]
    for o in range(1, chips):
        total_square += ss_recv[o]
    scale = lax.rsqrt(total_square / features + 1e-06)[:, 0:1]
    for c in range(parts):
        total = own[c]
        for o in range(1, chips):
            p_copies[c * (chips - 1) + o - 1].wait()
            total += precv[c, o].astype(F32)
        for i, base in enumerate((0, half)):
            result = total[i * tokens_local:(i + 1) * tokens_local, :] * scale
            at = slice(base + c * tile, base + (c + 1) * tile)
            for r in range(rows_local):
                out_ref[r, :, at] = result[r * steps:(r + 1) * steps, :].astype(BF16)


def fused(
    queries, keys, values, gate_input, decay_rate, norm_gain, out_weight, prompt_states, group_sizes
):
    chips = lax.axis_size("replica") // 2
    rows_local, steps, features = queries.shape
    prompts, share, hd = prompt_states.shape
    width = out_weight.shape[1]
    tokens_local = rows_local * steps
    parts = 2
    tile = width // 2 // parts
    vmem = pl.BlockSpec(memory_space=pltpu.VMEM)
    smem = pl.BlockSpec(memory_space=pltpu.SMEM)
    hbm = pl.BlockSpec(memory_space=pl.ANY)
    dma = pltpu.SemaphoreType.DMA
    return pl.pallas_call(
        functools.partial(kernel, chips),
        out_shape=jax.ShapeDtypeStruct((rows_local, steps, width), BF16),
        in_specs=[vmem, vmem, vmem, vmem, smem, vmem, hbm, hbm, smem],
        out_specs=vmem,
        scratch_shapes=[
            pltpu.VMEM((4 * tokens_local, features), F32),
            pltpu.VMEM((chips, 4 * tokens_local, 2 * share), BF16),
            pltpu.VMEM((chips, 4 * tokens_local, 2 * share), BF16),
            pltpu.VMEM((2, share, width), BF16),
            pltpu.VMEM((2, prompts, share, hd), BF16),
            pltpu.VMEM((parts, chips, 2 * tokens_local, tile), BF16),
            pltpu.VMEM((parts, chips, 2 * tokens_local, tile), BF16),
            pltpu.VMEM((parts, 2 * tokens_local, tile), F32),
            pltpu.VMEM((chips, tokens_local, 128), F32),
            pltpu.VMEM((chips, tokens_local, 128), F32),
            dma((2,)), dma((2,)), dma((2,)),
            dma((chips,)), dma((chips,)),
            dma((parts, chips)), dma((parts, chips)),
            dma((chips,)), dma((chips,)),
        ],
        compiler_params=pltpu.CompilerParams(
            collective_id=0, has_side_effects=True, vmem_limit_bytes=48 * 1024 * 1024
        ),
    )(
        queries, keys, values, gate_input, decay_rate, norm_gain.reshape(-1, hd),
        out_weight, prompt_states, group_sizes,
    )


def general(
    queries, keys, values, gate_input, decay_rate, norm_gain, out_weight, prompt_states, group_sizes
):
    replicas = lax.axis_size("replica")
    rows_local, steps_count, features = queries.shape
    head_size = prompt_states.shape[2]
    head_count = features // head_size
    share = prompt_states.shape[1]
    rows_total = rows_local * replicas
    ends = jnp.cumsum(group_sizes)
    row_ids = jnp.arange(rows_total, dtype=jnp.int32)
    owners = jnp.sum((row_ids[:, None] >= ends[None, :]).astype(jnp.int32), axis=1)
    q_four = queries.reshape(rows_local, steps_count, head_count, head_size)
    k_four = keys.reshape(rows_local, steps_count, head_count, head_size)
    v_four = values.astype(F32).reshape(rows_local, steps_count, head_count, head_size)
    piece = min(share, head_size)
    pieces_here = share // piece
    per_head = head_size // piece
    query_parts = queries.reshape(rows_local, steps_count, replicas, share)
    held_queries = lax.all_to_all(query_parts, "replica", split_axis=2, concat_axis=0, tiled=True)
    held_queries = held_queries.reshape(rows_total, steps_count, pieces_here, piece)
    held_states = jnp.take(prompt_states, owners, axis=0).reshape(
        rows_total, pieces_here, piece, head_size
    )
    partial_value = jnp.einsum(
        "rtcd,rcde->rtce", held_queries, held_states, preferred_element_type=F32
    )
    partial_value = partial_value.reshape(replicas, rows_local, steps_count, pieces_here, head_size)
    returned = lax.all_to_all(partial_value, "replica", split_axis=0, concat_axis=0, tiled=True)
    returned = jnp.moveaxis(returned, 0, 2)
    returned = returned.reshape(rows_local, steps_count, head_count, per_head, head_size)
    prompt_read = jnp.sum(returned, axis=3)
    times = jnp.arange(1, steps_count + 1).astype(F32)
    lead = jnp.exp(-times[:, None] * decay_rate[None, :])
    gap = times[:, None] - times[None, :]
    weights_mix = jnp.where(
        gap[None] >= 0.0, jnp.exp(-jnp.maximum(gap, 0.0)[None] * decay_rate[:, None, None]), 0.0
    )
    scores = jnp.einsum("rthd,rshd->rhts", q_four, k_four, preferred_element_type=F32)
    recent = jnp.einsum(
        "rhts,rshe->rthe", scores * weights_mix[None], v_four, precision=lax.Precision.HIGHEST
    )
    attention = lead[None, :, :, None] * prompt_read + recent
    attention = attention.reshape(rows_local, steps_count, features)
    mean_square = jnp.mean(attention * attention, axis=-1, keepdims=True)
    gate = jax.nn.sigmoid(gate_input.astype(F32))
    hidden = (attention * lax.rsqrt(mean_square + 1e-06) * norm_gain * gate).astype(BF16)
    hidden = hidden.reshape(rows_local * steps_count, features)
    columns_held = lax.all_to_all(hidden, "replica", split_axis=1, concat_axis=0, tiled=True)
    sums = jnp.dot(columns_held, out_weight, preferred_element_type=F32)
    sums = sums.reshape(replicas, rows_local * steps_count, out_weight.shape[1])
    sums = lax.all_to_all(sums, "replica", split_axis=0, concat_axis=0, tiled=True)
    mixed = jnp.sum(sums, axis=0)
    return mixed.astype(BF16).reshape(rows_local, steps_count, out_weight.shape[1])


def on_device(*args):
    prompt_states = args[7]
    if prompt_states.shape[1] % prompt_states.shape[2] == 0:
        return fused(*args)
    return general(*args)


def solution(mesh):
    rows = P(("groups", "replica"), None, None)
    in_specs = (
        rows, rows, rows, rows, P(), P(), P("replica", None), P("groups", "replica", None), P("groups"),
    )
    return jax.shard_map(
        on_device, mesh=mesh, in_specs=in_specs, out_specs=rows, check_vma=False
    )
```

time: 115 us -> 33.2 us (0.29)
  waiting for transfers between devices: 66.4 us -> 0 us
  Pallas kernels: 0 us -> 24.4 us
  between operations: 13.5 us -> 0.02 us
  starting transfers between devices: 11.5 us -> 0 us
  blocking collectives: 9.48 us -> 0 us
  matrix products: 5.22 us -> 0 us
  other arithmetic: 2.95 us -> 0 us
  local copies, waits for them, and re-layouts: 5.53 us -> 8.36 us
    reduce_scatter x1 -> x0, waiting for transfers between devices: 57 us -> none  [on_device(): lax.psum_scatter(jnp.dot(columns_held, out_weight, preferred_element_type...]
    pallas_call x0 -> x1, Pallas kernels: none -> 24.4 us  [fused(): pl.pallas_call(functools.partial(kernel, chips), out_shape=jax.ShapeDtype...]
    all_to_all x2 -> x0, starting transfers between devices: 11.5 us -> none  [the longest x1 7.36 us: on_device(): lax.all_to_all(query_parts, 'replica', split_axis=2, concat_axis=0, tiled...]
    all_to_all x1 -> x0, blocking collectives: 9.48 us -> none  [on_device(): lax.all_to_all(hidden, 'replica', split_axis=1, concat_axis=0, tiled=True)]
    all_to_all x2 -> x0, waiting for transfers between devices: 9.42 us -> none  [the longest x1 7.49 us: on_device(): lax.all_to_all(partial_value, 'replica', split_axis=0, concat_axis=0, til...]
    unnamed x14 -> x19, local copies, waits for them, and re-layouts: 0.03 us -> 8.36 us
    dot_general x4 -> x0, matrix products: 5.22 us -> none  [the longest x1 3.02 us: on_device(): jnp.einsum('rtcd,rcde->rtce', held_queries, held_states, preferred_elemen...]
    gather x1 -> x0, local copies, waits for them, and re-layouts: 3.1 us -> none  [on_device(): jnp.take(prompt_states, owners, axis=0)]
  transfers between devices with their start and end apart: 3 -> 0, of which waited for: 3 -> 0; matrix products, arithmetic and copies ran while one was open for 5% -> 0% of each run, Pallas kernels for 0% -> 0%
where the time goes in v1:
time: 33.2 us; the launch traced here: 32.8 us
  Pallas kernels  24.4 us (73%)
  local copies, waits for them, and re-layouts  8.36 us (25%)
    pallas_call x1, Pallas kernels, fused(): pl.pallas_call(functools.partial(kernel, chips), out_shape=jax.ShapeDtype...  24.4 us
    unnamed x19, local copies, waits for them, and re-layouts  8.36 us

profile of v1, /device:TPU:0, one launch (start us, length us, event | category | flops | bytes accessed | tf_op | source)
XLA Modules:
  0.0 32.8 jit_solution(12393347596770587111)
XLA Ops:
  0.0 0.0 copy-start
  0.0 1.4 %copy-done = bf16[256,3072]{1,0:T(8,128)(2,1)S(1)} copy-done((bf16[256,3072]{1,0:T(8,128)(2,1)S(1)}, bf16[256,3072]{1,0:T(8,128)(2,1)}, u32[]{:S(2)}) %copy-start) | copy-done | bytes 1572888
  1.4 0.0 copy-start.1
  1.4 0.9 %copy-done.1 = bf16[4,256,128]{2,1,0:T(8,128)(2,1)S(1)} copy-done((bf16[4,256,128]{2,1,0:T(8,128)(2,1)S(1)}, bf16[4,256,128]{2,1,0:T(8,128)(2,1)}, u32[]{:S(2)}) %copy-start.1) | copy-done | bytes 262168
  2.4 0.0 copy-start.2
  2.4 0.8 %copy-done.2 = bf16[2,4,4096]{2,1,0:T(4,128)(2,1)S(1)} copy-done((bf16[2,4,4096]{2,1,0:T(4,128)(2,1)S(1)}, bf16[2,4,4096]{2,1,0:T(4,128)(2,1)}, u32[]{:S(2)}) %copy-start.2) | copy-done | bytes 65560
  3.2 0.0 copy-start.3
  3.2 0.8 %copy-done.3 = bf16[2,4,4096]{2,1,0:T(4,128)(2,1)S(1)} copy-done((bf16[2,4,4096]{2,1,0:T(4,128)(2,1)S(1)}, bf16[2,4,4096]{2,1,0:T(4,128)(2,1)}, u32[]{:S(2)}) %copy-start.3) | copy-done | bytes 65560
  4.0 0.0 copy-start.4
  4.0 0.8 %copy-done.4 = bf16[2,4,4096]{2,1,0:T(4,128)(2,1)S(1)} copy-done((bf16[2,4,4096]{2,1,0:T(4,128)(2,1)S(1)}, bf16[2,4,4096]{2,1,0:T(4,128)(2,1)}, u32[]{:S(2)}) %copy-start.4) | copy-done | bytes 65560
  4.9 0.0 copy-start.5
  4.9 0.8 %copy-done.5 = bf16[2,4,4096]{2,1,0:T(4,128)(2,1)S(1)} copy-done((bf16[2,4,4096]{2,1,0:T(4,128)(2,1)S(1)}, bf16[2,4,4096]{2,1,0:T(4,128)(2,1)}, u32[]{:S(2)}) %copy-start.5) | copy-done | bytes 65560
  5.7 0.0 copy-start.6
  5.7 0.7 %copy-done.6 = f32[4096]{0:T(1024)S(1)} copy-done((f32[4096]{0:T(1024)S(1)}, f32[4096]{0:T(1024)}, u32[]{:S(2)}) %copy-start.6) | copy-done | bytes 16408
  6.4 0.0 copy-start.7
  6.4 0.7 %copy-done.7 = f32[32]{0:T(128)S(1)} copy-done((f32[32]{0:T(128)S(1)}, f32[32]{0:T(128)}, u32[]{:S(2)}) %copy-start.7) | copy-done | bytes 152
  7.1 0.0 copy-start.8
  7.1 0.7 %copy-done.8 = s32[4]{0:T(128)S(1)} copy-done((s32[4]{0:T(128)S(1)}, s32[4]{0:T(128)}, u32[]{:S(2)}) %copy-start.8) | copy-done | bytes 40
  7.7 24.4 %shard_map.91 = bf16[2,4,3072]{2,1,0:T(4,128)(2,1)S(1)} custom-call(bf16[2,4,4096]{2,1,0:T(4,128)(2,1)S(1)} %copy-done.2, bf16[2,4,4096]{2,1,0:T(4,128)(2,1)S(1)} %copy-done.3, bf16[2,4,4096]{2,1,0:T(4,128)(2,1)S(1)} %copy-done.4, bf16[2,4,4096]{2,1,0:T(4,128)(2,1)S(1)} %copy-done.5, f32[32]{0:T(128)S(1)} %copy-done.7, f32[32,128]{1,0:T(8,128)S(1)} %bitcast.1, ...), custom_call_target="tpu_custom_call" | custom-call | tf_op jit(solution)/shard_map/pallas_call | solution.py:200
  32.2 0.6 %copy.11 = bf16[2,4,3072]{2,1,0:T(4,128)(2,1)} copy(bf16[2,4,3072]{2,1,0:T(4,128)(2,1)S(1)} %shard_map.91) | data formatting | bytes 98304
Async XLA Ops:
  0.0 1.4 %copy-start = (bf16[256,3072]{1,0:T(8,128)(2,1)S(1)}, bf16[256,3072]{1,0:T(8,128)(2,1)}, u32[]{:S(2)}) copy-start(bf16[256,3072]{1,0:T(8,128)(2,1)} %w_hbm.1) | copy-start | bytes 4718596
  1.4 0.9 %copy-start.1 = (bf16[4,256,128]{2,1,0:T(8,128)(2,1)S(1)}, bf16[4,256,128]{2,1,0:T(8,128)(2,1)}, u32[]{:S(2)}) copy-start(bf16[4,256,128]{2,1,0:T(8,128)(2,1)} %st_hbm.1) | copy-start | bytes 786436
  2.4 0.8 %copy-start.2 = (bf16[2,4,4096]{2,1,0:T(4,128)(2,1)S(1)}, bf16[2,4,4096]{2,1,0:T(4,128)(2,1)}, u32[]{:S(2)}) copy-start(bf16[2,4,4096]{2,1,0:T(4,128)(2,1)} %q_ref.1) | copy-start | bytes 196612
  3.2 0.8 %copy-start.3 = (bf16[2,4,4096]{2,1,0:T(4,128)(2,1)S(1)}, bf16[2,4,4096]{2,1,0:T(4,128)(2,1)}, u32[]{:S(2)}) copy-start(bf16[2,4,4096]{2,1,0:T(4,128)(2,1)} %k_ref.1) | copy-start | bytes 196612
  4.0 0.8 %copy-start.4 = (bf16[2,4,4096]{2,1,0:T(4,128)(2,1)S(1)}, bf16[2,4,4096]{2,1,0:T(4,128)(2,1)}, u32[]{:S(2)}) copy-start(bf16[2,4,4096]{2,1,0:T(4,128)(2,1)} %v_ref.1) | copy-start | bytes 196612
  4.9 0.8 %copy-start.5 = (bf16[2,4,4096]{2,1,0:T(4,128)(2,1)S(1)}, bf16[2,4,4096]{2,1,0:T(4,128)(2,1)}, u32[]{:S(2)}) copy-start(bf16[2,4,4096]{2,1,0:T(4,128)(2,1)} %g_ref.1) | copy-start | bytes 196612
  5.7 0.7 %copy-start.6 = (f32[4096]{0:T(1024)S(1)}, f32[4096]{0:T(1024)}, u32[]{:S(2)}) copy-start(f32[4096]{0:T(1024)} %param.14) | copy-start | bytes 49156
  6.4 0.7 %copy-start.7 = (f32[32]{0:T(128)S(1)}, f32[32]{0:T(128)}, u32[]{:S(2)}) copy-start(f32[32]{0:T(128)} %decay_ref.1) | copy-start | bytes 388
  7.1 0.7 %copy-start.8 = (s32[4]{0:T(128)S(1)}, s32[4]{0:T(128)}, u32[]{:S(2)}) copy-start(s32[4]{0:T(128)} %gs_ref.1) | copy-start | bytes 52

commit v2 on v1

--- a/solution.py
+++ b/solution.py
@@ -236,7 +236,9 @@
     head_count = features // head_size
     share = prompt_states.shape[1]
     rows_total = rows_local * replicas
-    ends = jnp.cumsum(group_sizes)
+    prompts = group_sizes.shape[0]
+    order = jnp.arange(prompts)
+    ends = jnp.sum(jnp.where(order[:, None] >= order[None, :], group_sizes[None, :], 0), axis=1)
     row_ids = jnp.arange(rows_total, dtype=jnp.int32)
     owners = jnp.sum((row_ids[:, None] >= ends[None, :]).astype(jnp.int32), axis=1)
     q_four = queries.reshape(rows_local, steps_count, head_count, head_size)
@@ -248,11 +250,15 @@
     query_parts = queries.reshape(rows_local, steps_count, replicas, share)
     held_queries = lax.all_to_all(query_parts, "replica", split_axis=2, concat_axis=0, tiled=True)
     held_queries = held_queries.reshape(rows_total, steps_count, pieces_here, piece)
-    held_states = jnp.take(prompt_states, owners, axis=0).reshape(
-        rows_total, pieces_here, piece, head_size
-    )
-    partial_value = jnp.einsum(
-        "rtcd,rcde->rtce", held_queries, held_states, preferred_element_type=F32
+    held_states = prompt_states.reshape(prompts, pieces_here, piece, head_size)
+
+    def add_prompt(p, so_far):
+        state = lax.dynamic_index_in_dim(held_states, p, 0, keepdims=False)
+        mine = jnp.where((owners == p)[:, None, None, None], held_queries, 0)
+        return so_far + jnp.einsum("rtcd,cde->rtce", mine, state, preferred_element_type=F32)
+
+    partial_value = lax.fori_loop(
+        0, prompts, add_prompt, jnp.zeros((rows_total, steps_count, pieces_here, head_size), F32)
     )
     partial_value = partial_value.reshape(replicas, rows_local, steps_count, pieces_here, head_size)
     returned = lax.all_to_all(partial_value, "replica", split_axis=0, concat_axis=0, tiled=True)

time: 33.2 us -> 33.2 us (level)
  no operation moved by 1% of the time
where the time goes in v2:
time: 33.2 us; the launch traced here: 32.8 us
  Pallas kernels  24.4 us (73%)
  local copies, waits for them, and re-layouts  8.36 us (25%)
    pallas_call x1, Pallas kernels, fused(): pl.pallas_call(functools.partial(kernel, chips), out_shape=jax.ShapeDtype...  24.4 us
    unnamed x19, local copies, waits for them, and re-layouts  8.36 us

profile of v2, /device:TPU:0, one launch (start us, length us, event | category | flops | bytes accessed | tf_op | source)
XLA Modules:
  0.0 32.8 jit_solution(12393347596770587111)
XLA Ops:
  0.0 0.0 copy-start
  0.0 1.4 %copy-done = bf16[256,3072]{1,0:T(8,128)(2,1)S(1)} copy-done((bf16[256,3072]{1,0:T(8,128)(2,1)S(1)}, bf16[256,3072]{1,0:T(8,128)(2,1)}, u32[]{:S(2)}) %copy-start) | copy-done | bytes 1572888
  1.4 0.0 copy-start.1
  1.4 0.9 %copy-done.1 = bf16[4,256,128]{2,1,0:T(8,128)(2,1)S(1)} copy-done((bf16[4,256,128]{2,1,0:T(8,128)(2,1)S(1)}, bf16[4,256,128]{2,1,0:T(8,128)(2,1)}, u32[]{:S(2)}) %copy-start.1) | copy-done | bytes 262168
  2.4 0.0 copy-start.2
  2.4 0.8 %copy-done.2 = bf16[2,4,4096]{2,1,0:T(4,128)(2,1)S(1)} copy-done((bf16[2,4,4096]{2,1,0:T(4,128)(2,1)S(1)}, bf16[2,4,4096]{2,1,0:T(4,128)(2,1)}, u32[]{:S(2)}) %copy-start.2) | copy-done | bytes 65560
  3.2 0.0 copy-start.3
  3.2 0.8 %copy-done.3 = bf16[2,4,4096]{2,1,0:T(4,128)(2,1)S(1)} copy-done((bf16[2,4,4096]{2,1,0:T(4,128)(2,1)S(1)}, bf16[2,4,4096]{2,1,0:T(4,128)(2,1)}, u32[]{:S(2)}) %copy-start.3) | copy-done | bytes 65560
  4.0 0.0 copy-start.4
  4.0 0.8 %copy-done.4 = bf16[2,4,4096]{2,1,0:T(4,128)(2,1)S(1)} copy-done((bf16[2,4,4096]{2,1,0:T(4,128)(2,1)S(1)}, bf16[2,4,4096]{2,1,0:T(4,128)(2,1)}, u32[]{:S(2)}) %copy-start.4) | copy-done | bytes 65560
  4.9 0.0 copy-start.5
  4.9 0.8 %copy-done.5 = bf16[2,4,4096]{2,1,0:T(4,128)(2,1)S(1)} copy-done((bf16[2,4,4096]{2,1,0:T(4,128)(2,1)S(1)}, bf16[2,4,4096]{2,1,0:T(4,128)(2,1)}, u32[]{:S(2)}) %copy-start.5) | copy-done | bytes 65560
  5.7 0.0 copy-start.6
  5.7 0.7 %copy-done.6 = f32[4096]{0:T(1024)S(1)} copy-done((f32[4096]{0:T(1024)S(1)}, f32[4096]{0:T(1024)}, u32[]{:S(2)}) %copy-start.6) | copy-done | bytes 16408
  6.4 0.0 copy-start.7
  6.4 0.7 %copy-done.7 = f32[32]{0:T(128)S(1)} copy-done((f32[32]{0:T(128)S(1)}, f32[32]{0:T(128)}, u32[]{:S(2)}) %copy-start.7) | copy-done | bytes 152
  7.1 0.0 copy-start.8
  7.1 0.7 %copy-done.8 = s32[4]{0:T(128)S(1)} copy-done((s32[4]{0:T(128)S(1)}, s32[4]{0:T(128)}, u32[]{:S(2)}) %copy-start.8) | copy-done | bytes 40
  7.7 24.4 %shard_map.91 = bf16[2,4,3072]{2,1,0:T(4,128)(2,1)S(1)} custom-call(bf16[2,4,4096]{2,1,0:T(4,128)(2,1)S(1)} %copy-done.2, bf16[2,4,4096]{2,1,0:T(4,128)(2,1)S(1)} %copy-done.3, bf16[2,4,4096]{2,1,0:T(4,128)(2,1)S(1)} %copy-done.4, bf16[2,4,4096]{2,1,0:T(4,128)(2,1)S(1)} %copy-done.5, f32[32]{0:T(128)S(1)} %copy-done.7, f32[32,128]{1,0:T(8,128)S(1)} %bitcast.1, ...), custom_call_target="tpu_custom_call" | custom-call | tf_op jit(solution)/shard_map/pallas_call | solution.py:200
  32.2 0.6 %copy.11 = bf16[2,4,3072]{2,1,0:T(4,128)(2,1)} copy(bf16[2,4,3072]{2,1,0:T(4,128)(2,1)S(1)} %shard_map.91) | data formatting | bytes 98304
Async XLA Ops:
  0.0 1.4 %copy-start = (bf16[256,3072]{1,0:T(8,128)(2,1)S(1)}, bf16[256,3072]{1,0:T(8,128)(2,1)}, u32[]{:S(2)}) copy-start(bf16[256,3072]{1,0:T(8,128)(2,1)} %w_hbm.1) | copy-start | bytes 4718596
  1.4 0.9 %copy-start.1 = (bf16[4,256,128]{2,1,0:T(8,128)(2,1)S(1)}, bf16[4,256,128]{2,1,0:T(8,128)(2,1)}, u32[]{:S(2)}) copy-start(bf16[4,256,128]{2,1,0:T(8,128)(2,1)} %st_hbm.1) | copy-start | bytes 786436
  2.4 0.8 %copy-start.2 = (bf16[2,4,4096]{2,1,0:T(4,128)(2,1)S(1)}, bf16[2,4,4096]{2,1,0:T(4,128)(2,1)}, u32[]{:S(2)}) copy-start(bf16[2,4,4096]{2,1,0:T(4,128)(2,1)} %q_ref.1) | copy-start | bytes 196612
  3.2 0.8 %copy-start.3 = (bf16[2,4,4096]{2,1,0:T(4,128)(2,1)S(1)}, bf16[2,4,4096]{2,1,0:T(4,128)(2,1)}, u32[]{:S(2)}) copy-start(bf16[2,4,4096]{2,1,0:T(4,128)(2,1)} %k_ref.1) | copy-start | bytes 196612
  4.0 0.8 %copy-start.4 = (bf16[2,4,4096]{2,1,0:T(4,128)(2,1)S(1)}, bf16[2,4,4096]{2,1,0:T(4,128)(2,1)}, u32[]{:S(2)}) copy-start(bf16[2,4,4096]{2,1,0:T(4,128)(2,1)} %v_ref.1) | copy-start | bytes 196612
  4.9 0.8 %copy-start.5 = (bf16[2,4,4096]{2,1,0:T(4,128)(2,1)S(1)}, bf16[2,4,4096]{2,1,0:T(4,128)(2,1)}, u32[]{:S(2)}) copy-start(bf16[2,4,4096]{2,1,0:T(4,128)(2,1)} %g_ref.1) | copy-start | bytes 196612
  5.7 0.7 %copy-start.6 = (f32[4096]{0:T(1024)S(1)}, f32[4096]{0:T(1024)}, u32[]{:S(2)}) copy-start(f32[4096]{0:T(1024)} %param.14) | copy-start | bytes 49156
  6.4 0.7 %copy-start.7 = (f32[32]{0:T(128)S(1)}, f32[32]{0:T(128)}, u32[]{:S(2)}) copy-start(f32[32]{0:T(128)} %decay_ref.1) | copy-start | bytes 388
  7.1 0.7 %copy-start.8 = (s32[4]{0:T(128)S(1)}, s32[4]{0:T(128)}, u32[]{:S(2)}) copy-start(s32[4]{0:T(128)} %gs_ref.1) | copy-start | bytes 52

commit v3 on v2

--- a/solution.py
+++ b/solution.py
@@ -14,9 +14,9 @@
 
 def kernel(
     chips,
-    q_ref, k_ref, v_ref, g_ref, decay_ref, gain_ref, w_hbm, st_hbm, gs_ref,
-    out_ref,
-    stage, sbuf, rbuf, w_buf, st_buf, pbuf, precv, own, ss_send, ss_recv,
+    q_hbm, k_hbm, v_hbm, g_hbm, decay_hbm, gain_hbm, w_hbm, st_hbm, gs_hbm,
+    out_hbm,
+    q_ref, k_ref, v_ref, g_ref, decay_ref, gain_ref, gs_ref, out_ref, stage, sbuf, rbuf, w_buf, st_buf, pbuf, precv, own, ss_send, ss_recv,
     local_sem, pair_send, pair_recv, x_send, x_recv, p_send, p_recv, s_send, s_recv,
 ):
     rows_local, steps, features = q_ref.shape
@@ -36,6 +36,15 @@
 
     w_own = pltpu.make_async_copy(w_hbm, w_buf.at[core], local_sem.at[0])
     st_own = pltpu.make_async_copy(st_hbm, st_buf.at[core], local_sem.at[1])
+    loads = [
+        pltpu.make_async_copy(src, dst, local_sem.at[2 + i])
+        for i, (src, dst) in enumerate((
+            (q_hbm, q_ref), (k_hbm, k_ref), (v_hbm, v_ref), (g_hbm, g_ref),
+            (decay_hbm, decay_ref), (gs_hbm, gs_ref), (gain_hbm, gain_ref),
+        ))
+    ]
+    for load in loads:
+        load.start()
     st_own.start()
     w_own.start()
 
@@ -45,6 +54,7 @@
         pl.semaphore_signal(barrier, inc=1, device_id=peer(chip + o), device_id_type=MESH)
 
     for kind, ref in enumerate((q_ref, k_ref, v_ref, g_ref)):
+        loads[kind].wait()
         for r in range(rows_local):
             at = kind * tokens_local + r * steps
             stage[at:at + steps, :] = ref[r].astype(F32)
@@ -86,6 +96,8 @@
     si = lax.broadcasted_iota(jnp.int32, (tokens, tokens), 1)
     live = (ti // steps == si // steps) & (si <= ti)
     gap = jnp.maximum(ti - si, 0).astype(F32)
+    for load in loads[4:]:
+        load.wait()
     masks = []
     start = jnp.int32(0)
     for p in range(prompts):
@@ -181,6 +193,9 @@
             at = slice(base + c * tile, base + (c + 1) * tile)
             for r in range(rows_local):
                 out_ref[r, :, at] = result[r * steps:(r + 1) * steps, :].astype(BF16)
+    stored = pltpu.make_async_copy(out_ref, out_hbm, local_sem.at[0])
+    stored.start()
+    stored.wait()
 
 
 def fused(
@@ -193,16 +208,19 @@
     tokens_local = rows_local * steps
     parts = 2
     tile = width // 2 // parts
-    vmem = pl.BlockSpec(memory_space=pltpu.VMEM)
-    smem = pl.BlockSpec(memory_space=pltpu.SMEM)
     hbm = pl.BlockSpec(memory_space=pl.ANY)
     dma = pltpu.SemaphoreType.DMA
     return pl.pallas_call(
         functools.partial(kernel, chips),
         out_shape=jax.ShapeDtypeStruct((rows_local, steps, width), BF16),
-        in_specs=[vmem, vmem, vmem, vmem, smem, vmem, hbm, hbm, smem],
-        out_specs=vmem,
+        in_specs=[hbm] * 9,
+        out_specs=hbm,
         scratch_shapes=[
+            *[pltpu.VMEM(queries.shape, BF16)] * 4,
+            pltpu.SMEM(decay_rate.shape, F32),
+            pltpu.VMEM((features // hd, hd), F32),
+            pltpu.SMEM(group_sizes.shape, jnp.int32),
+            pltpu.VMEM((rows_local, steps, width), BF16),
             pltpu.VMEM((4 * tokens_local, features), F32),
             pltpu.VMEM((chips, 4 * tokens_local, 2 * share), BF16),
             pltpu.VMEM((chips, 4 * tokens_local, 2 * share), BF16),
@@ -213,13 +231,13 @@
             pltpu.VMEM((parts, 2 * tokens_local, tile), F32),
             pltpu.VMEM((chips, tokens_local, 128), F32),
             pltpu.VMEM((chips, tokens_local, 128), F32),
-            dma((2,)), dma((2,)), dma((2,)),
+            dma((9,)), dma((2,)), dma((2,)),
             dma((chips,)), dma((chips,)),
             dma((parts, chips)), dma((parts, chips)),
             dma((chips,)), dma((chips,)),
         ],
         compiler_params=pltpu.CompilerParams(
-            collective_id=0, has_side_effects=True, vmem_limit_bytes=48 * 1024 * 1024
+            collective_id=0, has_side_effects=True, vmem_limit_bytes=60 * 1024 * 1024
         ),
     )(
         queries, keys, values, gate_input, decay_rate, norm_gain.reshape(-1, hd),

time: 33.2 us -> 26 us (0.78)
  local copies, waits for them, and re-layouts: 8.36 us -> 1.44 us
    unnamed x19 -> x1, local copies, waits for them, and re-layouts: 8.36 us -> 1.44 us
where the time goes in v3:
time: 26 us; the launch traced here: 25.8 us
  Pallas kernels  24.4 us (94%)
  local copies, waits for them, and re-layouts  1.44 us (6%)
    pallas_call x1, Pallas kernels, fused(): pl.pallas_call(functools.partial(kernel, chips), out_shape=jax.ShapeDtype...  24.4 us
    unnamed x1, local copies, waits for them, and re-layouts  1.44 us

profile of v3, /device:TPU:0, one launch (start us, length us, event | category | flops | bytes accessed | tf_op | source)
XLA Modules:
  0.0 25.8 jit_solution(14082345048137391653)
XLA Ops:
  0.0 24.4 %shard_map.91 = bf16[2,4,3072]{2,1,0:T(4,128)(2,1)} custom-call(bf16[2,4,4096]{2,1,0:T(4,128)(2,1)} %q_hbm.1, bf16[2,4,4096]{2,1,0:T(4,128)(2,1)} %k_hbm.1, bf16[2,4,4096]{2,1,0:T(4,128)(2,1)} %v_hbm.1, bf16[2,4,4096]{2,1,0:T(4,128)(2,1)} %g_hbm.1, f32[32]{0:T(128)} %decay_hbm.1, f32[32,128]{1,0:T(8,128)} %bitcast.1, bf16[256,3072]{1,0:T(8,128)(2,1)} %w_hbm.1, ...), custom_call_target="tpu_custom_call" | custom-call | tf_op jit(solution)/shard_map/pallas_call | solution.py:213
  24.4 1.4 %copy.11 = bf16[2,4,3072]{2,1,0:T(4,128)(2,1)} copy(bf16[2,4,3072]{2,1,0:T(4,128)(2,1)} %shard_map.91) | data formatting | bytes 98304

commit v4 on v3

--- a/solution.py
+++ b/solution.py
@@ -15,8 +15,8 @@
 def kernel(
     chips,
     q_hbm, k_hbm, v_hbm, g_hbm, decay_hbm, gain_hbm, w_hbm, st_hbm, gs_hbm,
-    out_hbm,
-    q_ref, k_ref, v_ref, g_ref, decay_ref, gain_ref, gs_ref, out_ref, stage, sbuf, rbuf, w_buf, st_buf, pbuf, precv, own, ss_send, ss_recv,
+    out_ref,
+    q_ref, k_ref, v_ref, g_ref, decay_ref, gain_ref, gs_ref, stage, sbuf, rbuf, w_buf, st_buf, pbuf, precv, own, ss_send, ss_recv,
     local_sem, pair_send, pair_recv, x_send, x_recv, p_send, p_recv, s_send, s_recv,
 ):
     rows_local, steps, features = q_ref.shape
@@ -193,9 +193,6 @@
             at = slice(base + c * tile, base + (c + 1) * tile)
             for r in range(rows_local):
                 out_ref[r, :, at] = result[r * steps:(r + 1) * steps, :].astype(BF16)
-    stored = pltpu.make_async_copy(out_ref, out_hbm, local_sem.at[0])
-    stored.start()
-    stored.wait()
 
 
 def fused(
@@ -214,13 +211,12 @@
         functools.partial(kernel, chips),
         out_shape=jax.ShapeDtypeStruct((rows_local, steps, width), BF16),
         in_specs=[hbm] * 9,
-        out_specs=hbm,
+        out_specs=pl.BlockSpec(memory_space=pltpu.VMEM),
         scratch_shapes=[
             *[pltpu.VMEM(queries.shape, BF16)] * 4,
             pltpu.SMEM(decay_rate.shape, F32),
             pltpu.VMEM((features // hd, hd), F32),
             pltpu.SMEM(group_sizes.shape, jnp.int32),
-            pltpu.VMEM((rows_local, steps, width), BF16),
             pltpu.VMEM((4 * tokens_local, features), F32),
             pltpu.VMEM((chips, 4 * tokens_local, 2 * share), BF16),
             pltpu.VMEM((chips, 4 * tokens_local, 2 * share), BF16),

time: 26 us -> 26 us (level)
  no operation moved by 1% of the time
where the time goes in v4:
time: 26 us; the launch traced here: 25.8 us
  Pallas kernels  24.4 us (94%)
  local copies, waits for them, and re-layouts  1.44 us (6%)
    pallas_call x1, Pallas kernels, fused(): pl.pallas_call(functools.partial(kernel, chips), out_shape=jax.ShapeDtype...  24.4 us
    unnamed x1, local copies, waits for them, and re-layouts  1.44 us

profile of v4, /device:TPU:0, one launch (start us, length us, event | category | flops | bytes accessed | tf_op | source)
XLA Modules:
  0.0 25.8 jit_solution(17481146335697495663)
XLA Ops:
  0.0 24.4 %shard_map.91 = bf16[2,4,3072]{2,1,0:T(4,128)(2,1)} custom-call(bf16[2,4,4096]{2,1,0:T(4,128)(2,1)} %q_hbm.1, bf16[2,4,4096]{2,1,0:T(4,128)(2,1)} %k_hbm.1, bf16[2,4,4096]{2,1,0:T(4,128)(2,1)} %v_hbm.1, bf16[2,4,4096]{2,1,0:T(4,128)(2,1)} %g_hbm.1, f32[32]{0:T(128)} %decay_hbm.1, f32[32,128]{1,0:T(8,128)} %bitcast.1, bf16[256,3072]{1,0:T(8,128)(2,1)} %w_hbm.1, ...), custom_call_target="tpu_custom_call" | custom-call | tf_op jit(solution)/shard_map/pallas_call | solution.py:210
  24.4 1.4 %copy.11 = bf16[2,4,3072]{2,1,0:T(4,128)(2,1)} copy(bf16[2,4,3072]{2,1,0:T(4,128)(2,1)} %shard_map.91) | data formatting | bytes 98304

commit v5 on v4

--- a/solution.py
+++ b/solution.py
@@ -68,8 +68,9 @@
 
     pl.semaphore_wait(barrier, chips)
 
+    far_first = sorted(range(1, chips), key=lambda i: -min(i, chips - i))
     x_copies = []
-    for o in range(1, chips):
+    for o in far_first:
         copy = pltpu.make_async_remote_copy(
             src_ref=sbuf.at[o], dst_ref=rbuf.at[o], send_sem=x_send.at[o], recv_sem=x_recv.at[o],
             device_id=peer(chip + o), device_id_type=MESH,
@@ -157,7 +158,7 @@
     w_own.wait()
     w_pair.wait()
     parts, tile = pbuf.shape[0], pbuf.shape[3]
-    p_copies = []
+    p_copies = {}
     for c in range(parts):
         pieces = []
         for base in (0, half):
@@ -168,14 +169,14 @@
         both = jnp.concatenate(pieces, axis=1)
         own[c] = both[0]
         pbuf[c] = both.astype(BF16)
-        for o in range(1, chips):
+        for o in far_first:
             copy = pltpu.make_async_remote_copy(
                 src_ref=pbuf.at[c, o], dst_ref=precv.at[c, o],
                 send_sem=p_send.at[c, o], recv_sem=p_recv.at[c, o],
                 device_id=peer(chip - o), device_id_type=MESH,
             )
             copy.start()
-            p_copies.append(copy)
+            p_copies[c, o] = copy
 
     for copy in s_copies:
         copy.wait()
@@ -186,7 +187,7 @@
     for c in range(parts):
         total = own[c]
         for o in range(1, chips):
-            p_copies[c * (chips - 1) + o - 1].wait()
+            p_copies[c, o].wait()
             total += precv[c, o].astype(F32)
         for i, base in enumerate((0, half)):
             result = total[i * tokens_local:(i + 1) * tokens_local, :] * scale

time: 26 us -> 25.5 us (0.981)
  Pallas kernels: 24.4 us -> 23.9 us
    pallas_call x1, Pallas kernels: 24.4 us -> 23.9 us  [fused(): pl.pallas_call(functools.partial(kernel, chips), out_shape=jax.ShapeDtype...]
where the time goes in v5:
time: 25.5 us; the launch traced here: 25.3 us
  Pallas kernels  23.9 us (94%)
  local copies, waits for them, and re-layouts  1.44 us (6%)
    pallas_call x1, Pallas kernels, fused(): pl.pallas_call(functools.partial(kernel, chips), out_shape=jax.ShapeDtype...  23.9 us
    unnamed x1, local copies, waits for them, and re-layouts  1.44 us

profile of v5, /device:TPU:0, one launch (start us, length us, event | category | flops | bytes accessed | tf_op | source)
XLA Modules:
  0.0 25.3 jit_solution(7640683469959776417)
XLA Ops:
  0.0 23.9 %shard_map.91 = bf16[2,4,3072]{2,1,0:T(4,128)(2,1)} custom-call(bf16[2,4,4096]{2,1,0:T(4,128)(2,1)} %q_hbm.1, bf16[2,4,4096]{2,1,0:T(4,128)(2,1)} %k_hbm.1, bf16[2,4,4096]{2,1,0:T(4,128)(2,1)} %v_hbm.1, bf16[2,4,4096]{2,1,0:T(4,128)(2,1)} %g_hbm.1, f32[32]{0:T(128)} %decay_hbm.1, f32[32,128]{1,0:T(8,128)} %bitcast.1, bf16[256,3072]{1,0:T(8,128)(2,1)} %w_hbm.1, ...), custom_call_target="tpu_custom_call" | custom-call | tf_op jit(solution)/shard_map/pallas_call | solution.py:211
  23.9 1.4 %copy.11 = bf16[2,4,3072]{2,1,0:T(4,128)(2,1)} copy(bf16[2,4,3072]{2,1,0:T(4,128)(2,1)} %shard_map.91) | data formatting | bytes 98304

commit v6 on v5

--- a/solution.py
+++ b/solution.py
@@ -16,8 +16,8 @@
     chips,
     q_hbm, k_hbm, v_hbm, g_hbm, decay_hbm, gain_hbm, w_hbm, st_hbm, gs_hbm,
     out_ref,
-    q_ref, k_ref, v_ref, g_ref, decay_ref, gain_ref, gs_ref, stage, sbuf, rbuf, w_buf, st_buf, pbuf, precv, own, ss_send, ss_recv,
-    local_sem, pair_send, pair_recv, x_send, x_recv, p_send, p_recv, s_send, s_recv,
+    q_ref, k_ref, v_ref, g_ref, decay_ref, gain_ref, gs_ref, stage, sbuf, rbuf, w_buf, st_buf, sums, side_send, side_recv, pbuf, precv, own, ss_send, ss_recv,
+    local_sem, pair_send, pair_recv, x_send, x_recv, p_send, p_recv, s_send, s_recv, c_send, c_recv,
 ):
     rows_local, steps, features = q_ref.shape
     tokens_local = rows_local * steps
@@ -157,8 +157,10 @@
     u1 = jnp.concatenate(us[heads_device:], axis=1)
     w_own.wait()
     w_pair.wait()
-    parts, tile = pbuf.shape[0], pbuf.shape[3]
-    p_copies = {}
+    parts, _, _, tile = sums.shape
+    lines = chips // 2
+    parity = lax.rem(chip, 2)
+    side_copies = []
     for c in range(parts):
         pieces = []
         for base in (0, half):
@@ -167,16 +169,34 @@
             y += jnp.dot(u1, w_buf[1, :, at], preferred_element_type=F32)
             pieces.append(y.reshape(chips, tokens_local, tile))
         both = jnp.concatenate(pieces, axis=1)
-        own[c] = both[0]
-        pbuf[c] = both.astype(BF16)
-        for o in far_first:
+        for m in range(lines):
+            sums[c, m] = both[2 * m]
+            side_send[c, m] = both[2 * m + 1].astype(BF16)
+        copy = pltpu.make_async_remote_copy(
+            src_ref=side_send.at[c], dst_ref=side_recv.at[c],
+            send_sem=c_send.at[c], recv_sem=c_recv.at[c],
+            device_id=peer(chip + 1 - 2 * parity), device_id_type=MESH,
+        )
+        copy.start()
+        side_copies.append(copy)
+
+    line_first = sorted(range(1, lines), key=lambda i: -min(i, lines - i))
+    p_copies = {}
+    for c in range(parts):
+        side_copies[c].wait()
+        for m in line_first + [0]:
+            total = sums[c, m] + side_recv[c, lax.rem(m + lines - parity, lines)].astype(F32)
+            if m == 0:
+                own[c] = total
+                continue
+            pbuf[c, m] = total.astype(BF16)
             copy = pltpu.make_async_remote_copy(
-                src_ref=pbuf.at[c, o], dst_ref=precv.at[c, o],
-                send_sem=p_send.at[c, o], recv_sem=p_recv.at[c, o],
-                device_id=peer(chip - o), device_id_type=MESH,
+                src_ref=pbuf.at[c, m], dst_ref=precv.at[c, m],
+                send_sem=p_send.at[c, m], recv_sem=p_recv.at[c, m],
+                device_id=peer(chip - 2 * m), device_id_type=MESH,
             )
             copy.start()
-            p_copies[c, o] = copy
+            p_copies[c, m] = copy
 
     for copy in s_copies:
         copy.wait()
@@ -186,9 +206,9 @@
     scale = lax.rsqrt(total_square / features + 1e-06)[:, 0:1]
     for c in range(parts):
         total = own[c]
-        for o in range(1, chips):
-            p_copies[c, o].wait()
-            total += precv[c, o].astype(F32)
+        for m in range(1, lines):
+            p_copies[c, m].wait()
+            total += precv[c, m].astype(F32)
         for i, base in enumerate((0, half)):
             result = total[i * tokens_local:(i + 1) * tokens_local, :] * scale
             at = slice(base + c * tile, base + (c + 1) * tile)
@@ -204,7 +224,7 @@
     prompts, share, hd = prompt_states.shape
     width = out_weight.shape[1]
     tokens_local = rows_local * steps
-    parts = 2
+    parts = 4
     tile = width // 2 // parts
     hbm = pl.BlockSpec(memory_space=pl.ANY)
     dma = pltpu.SemaphoreType.DMA
@@ -223,15 +243,18 @@
             pltpu.VMEM((chips, 4 * tokens_local, 2 * share), BF16),
             pltpu.VMEM((2, share, width), BF16),
             pltpu.VMEM((2, prompts, share, hd), BF16),
-            pltpu.VMEM((parts, chips, 2 * tokens_local, tile), BF16),
-            pltpu.VMEM((parts, chips, 2 * tokens_local, tile), BF16),
+            pltpu.VMEM((parts, chips // 2, 2 * tokens_local, tile), F32),
+            pltpu.VMEM((parts, chips // 2, 2 * tokens_local, tile), BF16),
+            pltpu.VMEM((parts, chips // 2, 2 * tokens_local, tile), BF16),
+            pltpu.VMEM((parts, chips // 2, 2 * tokens_local, tile), BF16),
+            pltpu.VMEM((parts, chips // 2, 2 * tokens_local, tile), BF16),
             pltpu.VMEM((parts, 2 * tokens_local, tile), F32),
             pltpu.VMEM((chips, tokens_local, 128), F32),
             pltpu.VMEM((chips, tokens_local, 128), F32),
             dma((9,)), dma((2,)), dma((2,)),
             dma((chips,)), dma((chips,)),
-            dma((parts, chips)), dma((parts, chips)),
-            dma((chips,)), dma((chips,)),
+            dma((parts, chips // 2)), dma((parts, chips // 2)),
+            dma((chips,)), dma((chips,)), dma((parts,)), dma((parts,)),
         ],
         compiler_params=pltpu.CompilerParams(
             collective_id=0, has_side_effects=True, vmem_limit_bytes=60 * 1024 * 1024
@@ -306,7 +329,8 @@
 
 def on_device(*args):
     prompt_states = args[7]
-    if prompt_states.shape[1] % prompt_states.shape[2] == 0:
+    aligned = prompt_states.shape[1] % prompt_states.shape[2] == 0
+    if aligned and lax.axis_size("replica") % 4 == 0:
         return fused(*args)
     return general(*args)
 

time: 25.5 us -> 25.8 us (1.012)
    pallas_call x1, Pallas kernels: 23.9 us -> 24.1 us  [fused(): pl.pallas_call(functools.partial(kernel, chips), out_shape=jax.ShapeDtype...]
where the time goes in v6:
time: 25.8 us; the launch traced here: 25.6 us
  Pallas kernels  24.1 us (93%)
  local copies, waits for them, and re-layouts  1.44 us (6%)
    pallas_call x1, Pallas kernels, fused(): pl.pallas_call(functools.partial(kernel, chips), out_shape=jax.ShapeDtype...  24.1 us
    unnamed x1, local copies, waits for them, and re-layouts  1.44 us

profile of v6, /device:TPU:0, one launch (start us, length us, event | category | flops | bytes accessed | tf_op | source)
XLA Modules:
  0.0 25.6 jit_solution(2010501939656377237)
XLA Ops:
  0.0 24.1 %shard_map.91 = bf16[2,4,3072]{2,1,0:T(4,128)(2,1)} custom-call(bf16[2,4,4096]{2,1,0:T(4,128)(2,1)} %q_hbm.1, bf16[2,4,4096]{2,1,0:T(4,128)(2,1)} %k_hbm.1, bf16[2,4,4096]{2,1,0:T(4,128)(2,1)} %v_hbm.1, bf16[2,4,4096]{2,1,0:T(4,128)(2,1)} %g_hbm.1, f32[32]{0:T(128)} %decay_hbm.1, f32[32,128]{1,0:T(8,128)} %bitcast.1, bf16[256,3072]{1,0:T(8,128)(2,1)} %w_hbm.1, ...), custom_call_target="tpu_custom_call" | custom-call | tf_op jit(solution)/shard_map/pallas_call | solution.py:231
  24.2 1.4 %copy.11 = bf16[2,4,3072]{2,1,0:T(4,128)(2,1)} copy(bf16[2,4,3072]{2,1,0:T(4,128)(2,1)} %shard_map.91) | data formatting | bytes 98304

commit v7 on v5

--- a/solution.py
+++ b/solution.py
@@ -34,6 +34,12 @@
     def peer(chip_index):
         return {"replica": lax.rem(chip_index + chips, chips) * 2 + core}
 
+    barrier = pltpu.get_barrier_semaphore()
+    far_first = sorted(range(1, chips), key=lambda i: -min(i, chips - i))
+    for o in far_first:
+        pl.semaphore_signal(barrier, inc=1, device_id=peer(chip + o), device_id_type=MESH)
+    pl.semaphore_signal(barrier, inc=1, device_id={"replica": partner}, device_id_type=MESH)
+
     w_own = pltpu.make_async_copy(w_hbm, w_buf.at[core], local_sem.at[0])
     st_own = pltpu.make_async_copy(st_hbm, st_buf.at[core], local_sem.at[1])
     loads = [
@@ -48,11 +54,6 @@
     st_own.start()
     w_own.start()
 
-    barrier = pltpu.get_barrier_semaphore()
-    pl.semaphore_signal(barrier, inc=1, device_id={"replica": partner}, device_id_type=MESH)
-    for o in range(1, chips):
-        pl.semaphore_signal(barrier, inc=1, device_id=peer(chip + o), device_id_type=MESH)
-
     for kind, ref in enumerate((q_ref, k_ref, v_ref, g_ref)):
         loads[kind].wait()
         for r in range(rows_local):
@@ -68,7 +69,6 @@
 
     pl.semaphore_wait(barrier, chips)
 
-    far_first = sorted(range(1, chips), key=lambda i: -min(i, chips - i))
     x_copies = []
     for o in far_first:
         copy = pltpu.make_async_remote_copy(

time: 25.5 us -> 25.5 us (level)
  no operation moved by 1% of the time
where the time goes in v7:
time: 25.5 us; the launch traced here: 25.3 us
  Pallas kernels  23.9 us (94%)
  local copies, waits for them, and re-layouts  1.44 us (6%)
    pallas_call x1, Pallas kernels, fused(): pl.pallas_call(functools.partial(kernel, chips), out_shape=jax.ShapeDtype...  23.9 us
    unnamed x1, local copies, waits for them, and re-layouts  1.44 us

profile of v7, /device:TPU:0, one launch (start us, length us, event | category | flops | bytes accessed | tf_op | source)
XLA Modules:
  0.0 25.3 jit_solution(10940963423094234470)
XLA Ops:
  0.0 23.9 %shard_map.91 = bf16[2,4,3072]{2,1,0:T(4,128)(2,1)} custom-call(bf16[2,4,4096]{2,1,0:T(4,128)(2,1)} %q_hbm.1, bf16[2,4,4096]{2,1,0:T(4,128)(2,1)} %k_hbm.1, bf16[2,4,4096]{2,1,0:T(4,128)(2,1)} %v_hbm.1, bf16[2,4,4096]{2,1,0:T(4,128)(2,1)} %g_hbm.1, f32[32]{0:T(128)} %decay_hbm.1, f32[32,128]{1,0:T(8,128)} %bitcast.1, bf16[256,3072]{1,0:T(8,128)(2,1)} %w_hbm.1, ...), custom_call_target="tpu_custom_call" | custom-call | tf_op jit(solution)/shard_map/pallas_call | solution.py:211
  23.9 1.4 %copy.11 = bf16[2,4,3072]{2,1,0:T(4,128)(2,1)} copy(bf16[2,4,3072]{2,1,0:T(4,128)(2,1)} %shard_map.91) | data formatting | bytes 98304
